TPU v7x, 512 devices: a whole 4x8x8 slice. The times are simulated.
512 devices in a mesh: row: 16 (over x, y_lo, core), col: 32 (over z, y_hi).
Axes of the slice: x: 4, y: 8 (y_hi: 4, y_lo: 2; y = y_hi * 2 + y_lo), z: 8, core: 2. Of those that a mesh axis runs over, the one named last changes fastest.
Arguments:
- eigvecs: float32 [4096, 4096], P('row', 'col'), may hold values from -6 to 6
- offsets: int32 [1], replicated, may hold values from 0 to 127
- plan: int32 [1, 30], replicated, may hold values from 0 to 31
- refl_v: float32 [32, 255, 128], P('col')
- refl_t: float32 [32, 128, 128], P('col'), as said below
Outputs:
- updated: float32 [4096, 4096], P('row', 'col')
Inputs may be any that keep to these rules, and one draw needn't show every extreme that they name: For each bank entry, I - refl_v refl_t refl_v^T is orthogonal up to rounding.
All inputs are finite; a program needn't handle non-finite values.
Results may differ from a plain program's by a relative error of at most 0.00015.
Values sent between devices are 32-bit elements; how exact they have to be, the bound alone decides.
A program may use at most 64 MiB of HBM per device.

v0:
```python
import jax
import jax.numpy as jnp
from jax import lax
from jax.sharding import PartitionSpec as P

HIGHEST = lax.Precision.HIGHEST


def from_root(value, axis, root):
    mine = lax.axis_index(axis) == root
    return lax.psum(jnp.where(mine, value, jnp.zeros_like(value)), axis)


def from_behind(value, axis, by):
    devices = lax.axis_size(axis)
    pairs = [(i, i + by) for i in range(devices) if 0 <= i + by < devices]
    return lax.ppermute(value, axis, pairs)


def apply_one(extended, row_start, vectors, factor, weight):
    span_rows = vectors.shape[0]
    block_rows = lax.dynamic_slice_in_dim(extended, row_start, span_rows, 0)
    inner_prod = jnp.dot(vectors.T, block_rows, precision=HIGHEST)
    scaled = jnp.dot(factor, inner_prod, precision=HIGHEST)
    block_rows = block_rows - weight * jnp.dot(vectors, scaled, precision=HIGHEST)
    return lax.dynamic_update_slice_in_dim(extended, block_rows, row_start, 0)


def on_device(eigvecs, offsets, plan, refl_v, refl_t):
    rows_dev = eigvecs.shape[0]
    band = refl_v.shape[2]
    span_rows = refl_v.shape[1]
    per_device = rows_dev // band
    bank_dev = refl_v.shape[0]
    row_count = lax.axis_size("row")
    my_row = lax.axis_index("row")
    sweep_count = offsets.shape[0]
    block_total = row_count * per_device - 2
    head_count = 2 * band
    padded_ids = jnp.pad(plan, ((0, 0), (0, 2)))
    my_ids = lax.dynamic_slice_in_dim(padded_ids, my_row * per_device, per_device, 1).reshape(-1)
    needed = sweep_count * per_device

    def fetch_block(index, stored):
        block_id = my_ids[index]
        owner_col = block_id // bank_dev
        owner_slot = block_id % bank_dev
        got_v, got_t = (
            from_root(refl_v[owner_slot], "col", owner_col),
            from_root(refl_t[owner_slot], "col", owner_col),
        )
        return (stored[0].at[index].set(got_v), stored[1].at[index].set(got_t))

    empty = (
        jnp.zeros((needed, span_rows, band), jnp.float32),
        jnp.zeros((needed, band, band), jnp.float32),
    )
    local_v, local_t = lax.fori_loop(0, needed, fetch_block, empty)
    tick_count = 2 * sweep_count - 2 + row_count

    def run_tick(tick, matrix):
        fetched = from_behind(matrix, "row", -1)
        lag = tick - my_row
        active = (lag >= 0) & (lag % 2 == 0) & (lag < 2 * sweep_count)
        sweep = jnp.clip(lag // 2, 0, sweep_count - 1)
        first_row = offsets[sweep]

        def process(current):
            extended = jnp.concatenate([current, fetched], 0)

            def apply_block(index, extended):
                row_start = first_row + index * band
                slot = sweep * per_device + index
                is_valid = (my_row * per_device + index < block_total).astype(jnp.float32)
                return apply_one(extended, row_start, local_v[slot], local_t[slot], is_valid)

            return lax.fori_loop(0, per_device, apply_block, extended)

        def unchanged(current):
            return jnp.concatenate([current, fetched], 0)

        extended = lax.cond(active, process, unchanged, matrix)
        returned = from_behind(extended[rows_dev:], "row", 1)
        sender_lag = lag + 1
        sender_live = (
            (my_row >= 1)
            & (sender_lag >= 0)
            & (sender_lag % 2 == 0)
            & (sender_lag < 2 * sweep_count)
        )
        matrix = extended[:rows_dev]
        new_head = jnp.where(sender_live, returned, matrix)
        return matrix.at[:head_count].set(new_head)

    return lax.fori_loop(0, tick_count, run_tick, eigvecs)


def solution(mesh):
    in_specs = (P("row", "col"), P(), P(), P("col", None, None), P("col", None, None))
    out_specs = P("row", "col")
    return jax.shard_map(
        on_device, mesh=mesh, in_specs=in_specs, out_specs=out_specs, check_vma=False
    )
```

profile of v0, /device:TPU:15, one launch (start us, length us, event | category | flops | bytes accessed | tf_op | source)
XLA Modules:
  0.0 997.5 jit_solution(11573870405648408309)
XLA Ops:
  8.3 602.7 %while.62 = (s32[]{:T(128)}, f32[2,255,128]{2,1,0:T(8,128)S(1)}, f32[2,128,128]{2,1,0:T(8,128)S(1)}, s32[2]{0:T(128)S(1)}, f32[1,255,128]{2,1,0:T(8,128)S(1)}, /...) while((s32[]{:T(128)}, f32[2,255,128]{2,1,0:T(8,128)S(1)}, ...), condition=%wide.region_4.5_spmd, body=%wide.region_0.4_spmd.sunk | while | flops 147094 | bytes 2421499 | solution.py:58
  11.6 290.2 %all-reduce.6.cloned.1.call-done = (f32[1,255,128]{2,1,0:T(8,128)}, f32[1,128,128]{2,1,0:T(8,128)}) async-done(((f32[1,255,128]{2,1,0:T(8,128)}, f32[1,128,128]{2,1,0:T(8,128)}), (f32[1,255,128]{2,1,0:T(8,128)}, f32[1,128,128]{2,1,0:T(8,128)})) %all-reduce.6.cloned.1.call-update) | async-done | bytes 196112 | tf_op jit(solution)/shard_map/while/body/eval_jaxpr/psum | solution.py:11
  301.8 1.5 select_dynamic-update-slice_fusion.4
  307.3 301.6 %all-reduce.6.cloned.1.call-done = (f32[1,255,128]{2,1,0:T(8,128)}, f32[1,128,128]{2,1,0:T(8,128)}) async-done(((f32[1,255,128]{2,1,0:T(8,128)}, f32[1,128,128]{2,1,0:T(8,128)}), (f32[1,255,128]{2,1,0:T(8,128)}, f32[1,128,128]{2,1,0:T(8,128)})) %all-reduce.6.cloned.1.call-update) | async-done | bytes 196112 | tf_op jit(solution)/shard_map/while/body/eval_jaxpr/psum | solution.py:11
  609.0 1.5 select_dynamic-update-slice_fusion.4
  611.1 378.9 %while.63 = (s32[]{:T(128)}, f32[256,128]{1,0:T(8,128)S(1)}, s32[]{:T(128)}, pred[]{:T(512)}, s32[1]{0:T(128)}, /*index=5*/f32[2,255,128]{2,1,0:T(8,128)S(1)}, f...) while((s32[]{:T(128)}, f32[256,128]{1,0:T(8,128)S(1)}, s32[]{:T(128)}, pred[]{:T(512)}, ...), condition=%wide.region_10.11_spmd, body=%wide.region_5.10_spmd.sunk | while | flops 125599528 | bytes 3472517 | solution.py:95
  611.1 23.0 %collective-permute-start = (f32[256,128]{1,0:T(8,128)S(1)}, f32[256,128]{1,0:T(8,128)S(1)}, u32[]{:S(2)}, u32[]{:S(2)}) collective-permute-start(f32[256,128]{1,0:T(8,128)S(1)} %get-tuple-element.970), channel_id=1, source_target_pairs={{32,0},{64,32},{96,64},{128,96},{160,128},{192,160},{224,192},{256... | collective-permute-start | bytes 393224 | tf_op jit(solution)/shard_map/while/body/eval_jaxpr/ppermute | solution.py:17
  638.1 3.0 collective-permute-done.1
  642.0 5.6 collective-permute-start
  650.2 1.3 collective-permute-start.1
  651.5 3.0 collective-permute-done.1
  655.4 5.6 collective-permute-start
  665.0 3.0 collective-permute-done.1
  668.9 5.6 collective-permute-start
  678.4 3.0 collective-permute-done.1
  682.3 6.4 collective-permute-start
  692.6 3.0 collective-permute-done.1
  696.5 6.5 collective-permute-start
  707.0 3.0 collective-permute-done.1
  710.9 6.5 collective-permute-start
  721.3 3.0 collective-permute-done.1
  725.2 6.5 collective-permute-start
  735.6 3.0 collective-permute-done.1
  739.5 6.5 collective-permute-start
  748.6 1.3 collective-permute-start.1
  749.9 9.7 collective-permute-done.1
  760.5 17.9 %collective-permute-start = (f32[256,128]{1,0:T(8,128)S(1)}, f32[256,128]{1,0:T(8,128)S(1)}, u32[]{:S(2)}, u32[]{:S(2)}) collective-permute-start(f32[256,128]{1,0:T(8,128)S(1)} %get-tuple-element.970), channel_id=1, source_target_pairs={{32,0},{64,32},{96,64},{128,96},{160,128},{192,160},{224,192},{256... | collective-permute-start | bytes 393224 | tf_op jit(solution)/shard_map/while/body/eval_jaxpr/ppermute | solution.py:17
  781.1 1.3 collective-permute-start.1
  782.4 11.7 %collective-permute-done.1 = f32[256,128]{1,0:T(8,128)S(1)} collective-permute-done((f32[256,128]{1,0:T(8,128)S(1)}, f32[256,128]{1,0:T(8,128)S(1)}, u32[]{:S(2)}, u32[]{:S(2)}) %collective-permute-start.1) | collective-permute-done | bytes 131104 | tf_op jit(solution)/shard_map/while/body/eval_jaxpr/ppermute | solution.py:17
  795.0 17.8 %collective-permute-start = (f32[256,128]{1,0:T(8,128)S(1)}, f32[256,128]{1,0:T(8,128)S(1)}, u32[]{:S(2)}, u32[]{:S(2)}) collective-permute-start(f32[256,128]{1,0:T(8,128)S(1)} %get-tuple-element.970), channel_id=1, source_target_pairs={{32,0},{64,32},{96,64},{128,96},{160,128},{192,160},{224,192},{256... | collective-permute-start | bytes 393224 | tf_op jit(solution)/shard_map/while/body/eval_jaxpr/ppermute | solution.py:17
  815.4 1.3 collective-permute-start.1
  816.7 11.9 %collective-permute-done.1 = f32[256,128]{1,0:T(8,128)S(1)} collective-permute-done((f32[256,128]{1,0:T(8,128)S(1)}, f32[256,128]{1,0:T(8,128)S(1)}, u32[]{:S(2)}, u32[]{:S(2)}) %collective-permute-start.1) | collective-permute-done | bytes 131104 | tf_op jit(solution)/shard_map/while/body/eval_jaxpr/ppermute | solution.py:17
  829.6 17.4 %collective-permute-start = (f32[256,128]{1,0:T(8,128)S(1)}, f32[256,128]{1,0:T(8,128)S(1)}, u32[]{:S(2)}, u32[]{:S(2)}) collective-permute-start(f32[256,128]{1,0:T(8,128)S(1)} %get-tuple-element.970), channel_id=1, source_target_pairs={{32,0},{64,32},{96,64},{128,96},{160,128},{192,160},{224,192},{256... | collective-permute-start | bytes 393224 | tf_op jit(solution)/shard_map/while/body/eval_jaxpr/ppermute | solution.py:17
  850.9 12.2 %collective-permute-done.1 = f32[256,128]{1,0:T(8,128)S(1)} collective-permute-done((f32[256,128]{1,0:T(8,128)S(1)}, f32[256,128]{1,0:T(8,128)S(1)}, u32[]{:S(2)}, u32[]{:S(2)}) %collective-permute-start.1) | collective-permute-done | bytes 131104 | tf_op jit(solution)/shard_map/while/body/eval_jaxpr/ppermute | solution.py:17
  864.0 17.2 %collective-permute-start = (f32[256,128]{1,0:T(8,128)S(1)}, f32[256,128]{1,0:T(8,128)S(1)}, u32[]{:S(2)}, u32[]{:S(2)}) collective-permute-start(f32[256,128]{1,0:T(8,128)S(1)} %get-tuple-element.970), channel_id=1, source_target_pairs={{32,0},{64,32},{96,64},{128,96},{160,128},{192,160},{224,192},{256... | collective-permute-start | bytes 393224 | tf_op jit(solution)/shard_map/while/body/eval_jaxpr/ppermute | solution.py:17
  885.2 12.5 %collective-permute-done.1 = f32[256,128]{1,0:T(8,128)S(1)} collective-permute-done((f32[256,128]{1,0:T(8,128)S(1)}, f32[256,128]{1,0:T(8,128)S(1)}, u32[]{:S(2)}, u32[]{:S(2)}) %collective-permute-start.1) | collective-permute-done | bytes 131104 | tf_op jit(solution)/shard_map/while/body/eval_jaxpr/ppermute | solution.py:17
  898.6 16.8 %collective-permute-start = (f32[256,128]{1,0:T(8,128)S(1)}, f32[256,128]{1,0:T(8,128)S(1)}, u32[]{:S(2)}, u32[]{:S(2)}) collective-permute-start(f32[256,128]{1,0:T(8,128)S(1)} %get-tuple-element.970), channel_id=1, source_target_pairs={{32,0},{64,32},{96,64},{128,96},{160,128},{192,160},{224,192},{256... | collective-permute-start | bytes 393224 | tf_op jit(solution)/shard_map/while/body/eval_jaxpr/ppermute | solution.py:17
  919.4 12.7 %collective-permute-done.1 = f32[256,128]{1,0:T(8,128)S(1)} collective-permute-done((f32[256,128]{1,0:T(8,128)S(1)}, f32[256,128]{1,0:T(8,128)S(1)}, u32[]{:S(2)}, u32[]{:S(2)}) %collective-permute-start.1) | collective-permute-done | bytes 131104 | tf_op jit(solution)/shard_map/while/body/eval_jaxpr/ppermute | solution.py:17
  933.1 16.7 %collective-permute-start = (f32[256,128]{1,0:T(8,128)S(1)}, f32[256,128]{1,0:T(8,128)S(1)}, u32[]{:S(2)}, u32[]{:S(2)}) collective-permute-start(f32[256,128]{1,0:T(8,128)S(1)} %get-tuple-element.970), channel_id=1, source_target_pairs={{32,0},{64,32},{96,64},{128,96},{160,128},{192,160},{224,192},{256... | collective-permute-start | bytes 393224 | tf_op jit(solution)/shard_map/while/body/eval_jaxpr/ppermute | solution.py:17
  953.7 13.0 %collective-permute-done.1 = f32[256,128]{1,0:T(8,128)S(1)} collective-permute-done((f32[256,128]{1,0:T(8,128)S(1)}, f32[256,128]{1,0:T(8,128)S(1)}, u32[]{:S(2)}, u32[]{:S(2)}) %collective-permute-start.1) | collective-permute-done | bytes 131104 | tf_op jit(solution)/shard_map/while/body/eval_jaxpr/ppermute | solution.py:17
  967.7 5.5 collective-permute-start
  974.1 10.8 %conditional.2 = (f32[512,128]{1,0:T(8,128)}) conditional(s32[]{:T(128)} %convert_element_type.21, (f32[256,128]{1,0:T(8,128)S(1)}, f32[256,128]{1,0:T(8,128)S(1)}) %tuple.149, (f32[256,128]{1,0:T(8,128)S(1)}, f32[256,128]{1,0:T(8,128)S(1)}, s32[1]{0:T(128)}, s32[]{:T(128)}, s32[]{:T(128)}, /*index=5*/s32[]{:T(128)}, pred[]{:T(512)}, ...), branch_computations={%region_6.6_spmd, %region_7.9_spmd} | conditional | flops 125566744 | bytes 1767995 | solution.py:82
  974.8 10.1 %while.61 = (s32[]{:T(128)}, f32[512,128]{1,0:T(8,128)}, s32[]{:T(128)}, s32[]{:T(128)}, s32[]{:T(128)}, /*index=5*/f32[2,255,128]{2,1,0:T(8,128)S(1)}, f32[2,12...) while((s32[]{:T(128)}, f32[512,128]{1,0:T(8,128)}, ...), condition=%wide.region_9.8_spmd, body=%wide.region_8.7_spmd.sunk | while | flops 125501192 | bytes 1243419 | solution.py:77
  975.5 1.3 fusion.30
  978.2 1.7 dynamic_update_slice.10
  980.5 1.3 fusion.30
  983.2 1.6 dynamic_update_slice.10
  987.1 1.9 collective-permute-done.1
  (129 shorter events, 93.7 us)
Async XLA Ops:
  6.5 0.9 copy-start.4
  6.5 0.7 copy-start.6
  7.5 0.8 copy-start.3
  7.5 0.8 copy-start.5
  8.3 602.8 %copy-start.1 = (f32[256,128]{1,0:T(8,128)S(1)}, f32[256,128]{1,0:T(8,128)}, u32[]{:S(2)}) copy-start(f32[256,128]{1,0:T(8,128)} %param.21) | copy-start | bytes 393220
  8.3 293.5 %all-reduce.6.cloned.1.call-start = ((), (), s32[]{:S(2)}) async-start(), calls=%async_computation | async-start | bytes 393216 | tf_op jit(solution)/shard_map/while/body/eval_jaxpr/psum | solution.py:11
  301.8 1.5 copy-start.2
  304.0 305.0 %all-reduce.6.cloned.1.call-start = ((), (), s32[]{:S(2)}) async-start(), calls=%async_computation | async-start | bytes 393216 | tf_op jit(solution)/shard_map/while/body/eval_jaxpr/psum | solution.py:11
  609.0 1.5 copy-start.2
  611.1 24.0 %collective-permute-start = (f32[256,128]{1,0:T(8,128)S(1)}, f32[256,128]{1,0:T(8,128)S(1)}, u32[]{:S(2)}, u32[]{:S(2)}) collective-permute-start(f32[256,128]{1,0:T(8,128)S(1)} %get-tuple-element.970), channel_id=1, source_target_pairs={{32,0},{64,32},{96,64},{128,96},{160,128},{192,160},{224,192},{256... | collective-permute-start | bytes 393224 | tf_op jit(solution)/shard_map/while/body/eval_jaxpr/ppermute | solution.py:17
  636.8 4.3 collective-permute-start.1
  642.0 6.6 collective-permute-start
  650.2 4.3 collective-permute-start.1
  655.4 6.6 collective-permute-start
  663.6 4.3 collective-permute-start.1
  668.9 6.6 collective-permute-start
  677.1 4.3 collective-permute-start.1
  682.3 7.4 collective-permute-start
  691.3 4.3 collective-permute-start.1
  696.5 7.5 collective-permute-start
  705.6 4.3 collective-permute-start.1
  710.9 7.5 collective-permute-start
  720.0 4.3 collective-permute-start.1
  725.2 7.5 collective-permute-start
  734.3 4.3 collective-permute-start.1
  739.5 7.5 collective-permute-start
  748.6 11.0 %collective-permute-start.1 = (f32[256,128]{1,0:T(8,128)S(1)}, f32[256,128]{1,0:T(8,128)S(1)}, u32[]{:S(2)}, u32[]{:S(2)}) collective-permute-start(f32[256,128]{1,0:T(8,128)S(1)} %slice.110), channel_id=1, source_target_pairs={{0,32},{32,64},{64,96},{96,128},{128,160},{160,192},{192,224},{224... | collective-permute-start | bytes 393224 | tf_op jit(solution)/shard_map/while/body/eval_jaxpr/ppermute | solution.py:17
  760.5 18.9 %collective-permute-start = (f32[256,128]{1,0:T(8,128)S(1)}, f32[256,128]{1,0:T(8,128)S(1)}, u32[]{:S(2)}, u32[]{:S(2)}) collective-permute-start(f32[256,128]{1,0:T(8,128)S(1)} %get-tuple-element.970), channel_id=1, source_target_pairs={{32,0},{64,32},{96,64},{128,96},{160,128},{192,160},{224,192},{256... | collective-permute-start | bytes 393224 | tf_op jit(solution)/shard_map/while/body/eval_jaxpr/ppermute | solution.py:17
  781.1 13.0 %collective-permute-start.1 = (f32[256,128]{1,0:T(8,128)S(1)}, f32[256,128]{1,0:T(8,128)S(1)}, u32[]{:S(2)}, u32[]{:S(2)}) collective-permute-start(f32[256,128]{1,0:T(8,128)S(1)} %slice.110), channel_id=1, source_target_pairs={{0,32},{32,64},{64,96},{96,128},{128,160},{160,192},{192,224},{224... | collective-permute-start | bytes 393224 | tf_op jit(solution)/shard_map/while/body/eval_jaxpr/ppermute | solution.py:17
  795.0 18.8 %collective-permute-start = (f32[256,128]{1,0:T(8,128)S(1)}, f32[256,128]{1,0:T(8,128)S(1)}, u32[]{:S(2)}, u32[]{:S(2)}) collective-permute-start(f32[256,128]{1,0:T(8,128)S(1)} %get-tuple-element.970), channel_id=1, source_target_pairs={{32,0},{64,32},{96,64},{128,96},{160,128},{192,160},{224,192},{256... | collective-permute-start | bytes 393224 | tf_op jit(solution)/shard_map/while/body/eval_jaxpr/ppermute | solution.py:17
  815.4 13.3 %collective-permute-start.1 = (f32[256,128]{1,0:T(8,128)S(1)}, f32[256,128]{1,0:T(8,128)S(1)}, u32[]{:S(2)}, u32[]{:S(2)}) collective-permute-start(f32[256,128]{1,0:T(8,128)S(1)} %slice.110), channel_id=1, source_target_pairs={{0,32},{32,64},{64,96},{96,128},{128,160},{160,192},{192,224},{224... | collective-permute-start | bytes 393224 | tf_op jit(solution)/shard_map/while/body/eval_jaxpr/ppermute | solution.py:17
  829.6 18.3 %collective-permute-start = (f32[256,128]{1,0:T(8,128)S(1)}, f32[256,128]{1,0:T(8,128)S(1)}, u32[]{:S(2)}, u32[]{:S(2)}) collective-permute-start(f32[256,128]{1,0:T(8,128)S(1)} %get-tuple-element.970), channel_id=1, source_target_pairs={{32,0},{64,32},{96,64},{128,96},{160,128},{192,160},{224,192},{256... | collective-permute-start | bytes 393224 | tf_op jit(solution)/shard_map/while/body/eval_jaxpr/ppermute | solution.py:17
  849.6 13.5 %collective-permute-start.1 = (f32[256,128]{1,0:T(8,128)S(1)}, f32[256,128]{1,0:T(8,128)S(1)}, u32[]{:S(2)}, u32[]{:S(2)}) collective-permute-start(f32[256,128]{1,0:T(8,128)S(1)} %slice.110), channel_id=1, source_target_pairs={{0,32},{32,64},{64,96},{96,128},{128,160},{160,192},{192,224},{224... | collective-permute-start | bytes 393224 | tf_op jit(solution)/shard_map/while/body/eval_jaxpr/ppermute | solution.py:17
  864.0 18.2 %collective-permute-start = (f32[256,128]{1,0:T(8,128)S(1)}, f32[256,128]{1,0:T(8,128)S(1)}, u32[]{:S(2)}, u32[]{:S(2)}) collective-permute-start(f32[256,128]{1,0:T(8,128)S(1)} %get-tuple-element.970), channel_id=1, source_target_pairs={{32,0},{64,32},{96,64},{128,96},{160,128},{192,160},{224,192},{256... | collective-permute-start | bytes 393224 | tf_op jit(solution)/shard_map/while/body/eval_jaxpr/ppermute | solution.py:17
  883.9 13.8 %collective-permute-start.1 = (f32[256,128]{1,0:T(8,128)S(1)}, f32[256,128]{1,0:T(8,128)S(1)}, u32[]{:S(2)}, u32[]{:S(2)}) collective-permute-start(f32[256,128]{1,0:T(8,128)S(1)} %slice.110), channel_id=1, source_target_pairs={{0,32},{32,64},{64,96},{96,128},{128,160},{160,192},{192,224},{224... | collective-permute-start | bytes 393224 | tf_op jit(solution)/shard_map/while/body/eval_jaxpr/ppermute | solution.py:17
  898.6 17.8 %collective-permute-start = (f32[256,128]{1,0:T(8,128)S(1)}, f32[256,128]{1,0:T(8,128)S(1)}, u32[]{:S(2)}, u32[]{:S(2)}) collective-permute-start(f32[256,128]{1,0:T(8,128)S(1)} %get-tuple-element.970), channel_id=1, source_target_pairs={{32,0},{64,32},{96,64},{128,96},{160,128},{192,160},{224,192},{256... | collective-permute-start | bytes 393224 | tf_op jit(solution)/shard_map/while/body/eval_jaxpr/ppermute | solution.py:17
  918.1 14.1 %collective-permute-start.1 = (f32[256,128]{1,0:T(8,128)S(1)}, f32[256,128]{1,0:T(8,128)S(1)}, u32[]{:S(2)}, u32[]{:S(2)}) collective-permute-start(f32[256,128]{1,0:T(8,128)S(1)} %slice.110), channel_id=1, source_target_pairs={{0,32},{32,64},{64,96},{96,128},{128,160},{160,192},{192,224},{224... | collective-permute-start | bytes 393224 | tf_op jit(solution)/shard_map/while/body/eval_jaxpr/ppermute | solution.py:17
  933.1 17.7 %collective-permute-start = (f32[256,128]{1,0:T(8,128)S(1)}, f32[256,128]{1,0:T(8,128)S(1)}, u32[]{:S(2)}, u32[]{:S(2)}) collective-permute-start(f32[256,128]{1,0:T(8,128)S(1)} %get-tuple-element.970), channel_id=1, source_target_pairs={{32,0},{64,32},{96,64},{128,96},{160,128},{192,160},{224,192},{256... | collective-permute-start | bytes 393224 | tf_op jit(solution)/shard_map/while/body/eval_jaxpr/ppermute | solution.py:17
  952.4 14.4 %collective-permute-start.1 = (f32[256,128]{1,0:T(8,128)S(1)}, f32[256,128]{1,0:T(8,128)S(1)}, u32[]{:S(2)}, u32[]{:S(2)}) collective-permute-start(f32[256,128]{1,0:T(8,128)S(1)} %slice.110), channel_id=1, source_target_pairs={{0,32},{32,64},{64,96},{96,128},{128,160},{160,192},{192,224},{224... | collective-permute-start | bytes 393224 | tf_op jit(solution)/shard_map/while/body/eval_jaxpr/ppermute | solution.py:17
  967.7 6.4 collective-permute-start
  985.8 3.2 collective-permute-start.1
  990.0 0.7 copy-start
Sparse Core Ops, SparseCore 0:
  12.1 289.6 all-reduce.5
  307.8 301.1 all-reduce.5
where the time goes:
time: 999 us; the launch traced here: 997 us
  waiting for transfers between devices  716 us (72%)
  starting transfers between devices  202 us (20%)
  other arithmetic  34.5 us (3%)
  local copies, waits for them, and re-layouts  21.5 us (2%)
  between operations  13.4 us (1%)
    psum x2, waiting for transfers between devices, from_root(): return lax.psum(jnp.where(mine, value, jnp.zeros_like(value)), axis)  592 us
    ppermute x32, starting transfers between devices, from_behind(): return lax.ppermute(value, axis, pairs)  202 us
    ppermute x32, waiting for transfers between devices, from_behind(): return lax.ppermute(value, axis, pairs)  124 us
  transfers between devices with their start and end apart: 34, of which 34 were waited for; matrix products, arithmetic and copies ran while one was open for 0% of the time, Pallas kernels for 0%

commit v1 on v0

--- a/solution.py
+++ b/solution.py
@@ -8,7 +8,7 @@
 
 def from_root(value, axis, root):
     mine = lax.axis_index(axis) == root
-    return lax.psum(jnp.where(mine, value, jnp.zeros_like(value)), axis)
+    return jnp.sum(lax.all_gather(jnp.where(mine, value, jnp.zeros_like(value)), axis), axis=0)
 
 
 def from_behind(value, axis, by):

time: 999 us -> 766 us (0.77)
  waiting for transfers between devices: 716 us -> 493 us
  starting transfers between devices: 202 us -> 183 us
    psum x2 -> x0, waiting for transfers between devices: 592 us -> none  [from_root(): return lax.psum(jnp.where(mine, value, jnp.zeros_like(value)), axis)]
    all_gather x0 -> x4, waiting for transfers between devices: none -> 369 us  [from_root(): lax.all_gather(jnp.where(mine, value, jnp.zeros_like(value)), axis)]
    ppermute x32, starting transfers between devices: 202 us -> 182 us  [from_behind(): return lax.ppermute(value, axis, pairs)]
  transfers between devices with their start and end apart: 34 -> 36, of which waited for: 34 -> 36; matrix products, arithmetic and copies ran while one was open for 0% -> 1% of each run, Pallas kernels for 0% -> 0%
where the time goes in v1:
time: 766 us; the launch traced here: 765 us
  waiting for transfers between devices  493 us (64%)
  starting transfers between devices  183 us (24%)
  other arithmetic  44.4 us (6%)
  local copies, waits for them, and re-layouts  21.4 us (3%)
  between operations  13.1 us (2%)
    all_gather x4, waiting for transfers between devices, from_root(): lax.all_gather(jnp.where(mine, value, jnp.zeros_like(value)), axis)  369 us
    ppermute x32, starting transfers between devices, from_behind(): return lax.ppermute(value, axis, pairs)  182 us
    ppermute x32, waiting for transfers between devices, from_behind(): return lax.ppermute(value, axis, pairs)  124 us
  transfers between devices with their start and end apart: 36, of which 36 were waited for; matrix products, arithmetic and copies ran while one was open for 1% of the time, Pallas kernels for 0%

profile of v1, /device:TPU:15, one launch (start us, length us, event | category | flops | bytes accessed | tf_op | source)
XLA Modules:
  0.0 764.5 jit_solution(6304886815237147952)
XLA Ops:
  8.2 389.8 %while.62 = (s32[]{:T(128)}, f32[2,255,128]{2,1,0:T(8,128)S(1)}, f32[2,128,128]{2,1,0:T(8,128)S(1)}, s32[2]{0:T(128)S(1)}, f32[1,255,128]{2,1,0:T(8,128)S(1)}, /...) while((s32[]{:T(128)}, f32[2,255,128]{2,1,0:T(8,128)S(1)}, ...), condition=%wide.region_4.5_spmd, body=%wide.region_0.4_spmd.sunk | while | flops 1617814 | bytes 26883860 | solution.py:58
  9.5 1.5 broadcast_select_fusion.5
  13.2 86.3 %all-gather.5.cloned.1.call-done = f32[32,128,128]{2,1,0:T(8,128)} async-done(((f32[1,128,128]{2,1,0:T(8,128)}), f32[32,128,128]{2,1,0:T(8,128)}) %all-gather.5.cloned.1.call-update) | async-done | bytes 2097168 | tf_op jit(solution)/shard_map/while/body/eval_jaxpr/all_gather | solution.py:11
  99.5 1.7 reduce_sum.35
  101.9 101.8 %all-gather.3.cloned.1.call-done = f32[32,255,128]{2,1,0:T(8,128)} async-done(((f32[1,255,128]{2,1,0:T(8,128)}), f32[32,255,128]{2,1,0:T(8,128)}) %all-gather.3.cloned.1.call-update) | async-done | bytes 4177936 | tf_op jit(solution)/shard_map/while/body/eval_jaxpr/all_gather | solution.py:11
  203.7 2.4 reduce_sum.34
  208.1 1.5 broadcast_select_fusion.5
  211.8 79.1 %all-gather.5.cloned.1.call-done = f32[32,128,128]{2,1,0:T(8,128)} async-done(((f32[1,128,128]{2,1,0:T(8,128)}), f32[32,128,128]{2,1,0:T(8,128)}) %all-gather.5.cloned.1.call-update) | async-done | bytes 2097168 | tf_op jit(solution)/shard_map/while/body/eval_jaxpr/all_gather | solution.py:11
  290.9 1.7 reduce_sum.35
  293.3 101.6 %all-gather.3.cloned.1.call-done = f32[32,255,128]{2,1,0:T(8,128)} async-done(((f32[1,255,128]{2,1,0:T(8,128)}), f32[32,255,128]{2,1,0:T(8,128)}) %all-gather.3.cloned.1.call-update) | async-done | bytes 4177936 | tf_op jit(solution)/shard_map/while/body/eval_jaxpr/all_gather | solution.py:11
  394.9 2.4 reduce_sum.34
  398.1 359.2 %while.63 = (s32[]{:T(128)}, f32[256,128]{1,0:T(8,128)S(1)}, s32[]{:T(128)}, pred[]{:T(512)}, s32[1]{0:T(128)}, /*index=5*/f32[2,255,128]{2,1,0:T(8,128)S(1)}, f...) while((s32[]{:T(128)}, f32[256,128]{1,0:T(8,128)S(1)}, s32[]{:T(128)}, pred[]{:T(512)}, ...), condition=%wide.region_10.11_spmd, body=%wide.region_5.10_spmd.sunk | while | flops 125599528 | bytes 3472517 | solution.py:95
  398.1 2.9 collective-permute-start
  404.9 3.0 collective-permute-done.1
  408.8 5.6 collective-permute-start
  418.3 3.0 collective-permute-done.1
  422.2 5.6 collective-permute-start
  431.8 3.0 collective-permute-done.1
  435.7 5.8 collective-permute-start
  445.4 3.0 collective-permute-done.1
  449.3 6.5 collective-permute-start
  459.8 3.0 collective-permute-done.1
  463.7 6.5 collective-permute-start
  474.1 3.0 collective-permute-done.1
  478.0 6.5 collective-permute-start
  488.4 3.0 collective-permute-done.1
  492.3 6.5 collective-permute-start
  502.7 3.0 collective-permute-done.1
  506.6 6.5 collective-permute-start
  517.1 9.7 %collective-permute-done.1 = f32[256,128]{1,0:T(8,128)S(1)} collective-permute-done((f32[256,128]{1,0:T(8,128)S(1)}, f32[256,128]{1,0:T(8,128)S(1)}, u32[]{:S(2)}, u32[]{:S(2)}) %collective-permute-start.1) | collective-permute-done | bytes 131104 | tf_op jit(solution)/shard_map/while/body/eval_jaxpr/ppermute | solution.py:17
  527.7 17.9 %collective-permute-start = (f32[256,128]{1,0:T(8,128)S(1)}, f32[256,128]{1,0:T(8,128)S(1)}, u32[]{:S(2)}, u32[]{:S(2)}) collective-permute-start(f32[256,128]{1,0:T(8,128)S(1)} %get-tuple-element.967), channel_id=1, source_target_pairs={{32,0},{64,32},{96,64},{128,96},{160,128},{192,160},{224,192},{256... | collective-permute-start | bytes 393224 | tf_op jit(solution)/shard_map/while/body/eval_jaxpr/ppermute | solution.py:17
  549.6 11.7 %collective-permute-done.1 = f32[256,128]{1,0:T(8,128)S(1)} collective-permute-done((f32[256,128]{1,0:T(8,128)S(1)}, f32[256,128]{1,0:T(8,128)S(1)}, u32[]{:S(2)}, u32[]{:S(2)}) %collective-permute-start.1) | collective-permute-done | bytes 131104 | tf_op jit(solution)/shard_map/while/body/eval_jaxpr/ppermute | solution.py:17
  562.2 17.8 %collective-permute-start = (f32[256,128]{1,0:T(8,128)S(1)}, f32[256,128]{1,0:T(8,128)S(1)}, u32[]{:S(2)}, u32[]{:S(2)}) collective-permute-start(f32[256,128]{1,0:T(8,128)S(1)} %get-tuple-element.967), channel_id=1, source_target_pairs={{32,0},{64,32},{96,64},{128,96},{160,128},{192,160},{224,192},{256... | collective-permute-start | bytes 393224 | tf_op jit(solution)/shard_map/while/body/eval_jaxpr/ppermute | solution.py:17
  583.9 11.9 %collective-permute-done.1 = f32[256,128]{1,0:T(8,128)S(1)} collective-permute-done((f32[256,128]{1,0:T(8,128)S(1)}, f32[256,128]{1,0:T(8,128)S(1)}, u32[]{:S(2)}, u32[]{:S(2)}) %collective-permute-start.1) | collective-permute-done | bytes 131104 | tf_op jit(solution)/shard_map/while/body/eval_jaxpr/ppermute | solution.py:17
  596.8 17.4 %collective-permute-start = (f32[256,128]{1,0:T(8,128)S(1)}, f32[256,128]{1,0:T(8,128)S(1)}, u32[]{:S(2)}, u32[]{:S(2)}) collective-permute-start(f32[256,128]{1,0:T(8,128)S(1)} %get-tuple-element.967), channel_id=1, source_target_pairs={{32,0},{64,32},{96,64},{128,96},{160,128},{192,160},{224,192},{256... | collective-permute-start | bytes 393224 | tf_op jit(solution)/shard_map/while/body/eval_jaxpr/ppermute | solution.py:17
  618.1 12.2 %collective-permute-done.1 = f32[256,128]{1,0:T(8,128)S(1)} collective-permute-done((f32[256,128]{1,0:T(8,128)S(1)}, f32[256,128]{1,0:T(8,128)S(1)}, u32[]{:S(2)}, u32[]{:S(2)}) %collective-permute-start.1) | collective-permute-done | bytes 131104 | tf_op jit(solution)/shard_map/while/body/eval_jaxpr/ppermute | solution.py:17
  631.3 17.3 %collective-permute-start = (f32[256,128]{1,0:T(8,128)S(1)}, f32[256,128]{1,0:T(8,128)S(1)}, u32[]{:S(2)}, u32[]{:S(2)}) collective-permute-start(f32[256,128]{1,0:T(8,128)S(1)} %get-tuple-element.967), channel_id=1, source_target_pairs={{32,0},{64,32},{96,64},{128,96},{160,128},{192,160},{224,192},{256... | collective-permute-start | bytes 393224 | tf_op jit(solution)/shard_map/while/body/eval_jaxpr/ppermute | solution.py:17
  652.5 12.5 %collective-permute-done.1 = f32[256,128]{1,0:T(8,128)S(1)} collective-permute-done((f32[256,128]{1,0:T(8,128)S(1)}, f32[256,128]{1,0:T(8,128)S(1)}, u32[]{:S(2)}, u32[]{:S(2)}) %collective-permute-start.1) | collective-permute-done | bytes 131104 | tf_op jit(solution)/shard_map/while/body/eval_jaxpr/ppermute | solution.py:17
  665.9 16.8 %collective-permute-start = (f32[256,128]{1,0:T(8,128)S(1)}, f32[256,128]{1,0:T(8,128)S(1)}, u32[]{:S(2)}, u32[]{:S(2)}) collective-permute-start(f32[256,128]{1,0:T(8,128)S(1)} %get-tuple-element.967), channel_id=1, source_target_pairs={{32,0},{64,32},{96,64},{128,96},{160,128},{192,160},{224,192},{256... | collective-permute-start | bytes 393224 | tf_op jit(solution)/shard_map/while/body/eval_jaxpr/ppermute | solution.py:17
  686.7 12.8 %collective-permute-done.1 = f32[256,128]{1,0:T(8,128)S(1)} collective-permute-done((f32[256,128]{1,0:T(8,128)S(1)}, f32[256,128]{1,0:T(8,128)S(1)}, u32[]{:S(2)}, u32[]{:S(2)}) %collective-permute-start.1) | collective-permute-done | bytes 131104 | tf_op jit(solution)/shard_map/while/body/eval_jaxpr/ppermute | solution.py:17
  700.4 16.7 %collective-permute-start = (f32[256,128]{1,0:T(8,128)S(1)}, f32[256,128]{1,0:T(8,128)S(1)}, u32[]{:S(2)}, u32[]{:S(2)}) collective-permute-start(f32[256,128]{1,0:T(8,128)S(1)} %get-tuple-element.967), channel_id=1, source_target_pairs={{32,0},{64,32},{96,64},{128,96},{160,128},{192,160},{224,192},{256... | collective-permute-start | bytes 393224 | tf_op jit(solution)/shard_map/while/body/eval_jaxpr/ppermute | solution.py:17
  721.0 13.0 %collective-permute-done.1 = f32[256,128]{1,0:T(8,128)S(1)} collective-permute-done((f32[256,128]{1,0:T(8,128)S(1)}, f32[256,128]{1,0:T(8,128)S(1)}, u32[]{:S(2)}, u32[]{:S(2)}) %collective-permute-start.1) | collective-permute-done | bytes 131104 | tf_op jit(solution)/shard_map/while/body/eval_jaxpr/ppermute | solution.py:17
  735.0 5.5 collective-permute-start
  741.4 10.8 %conditional.2 = (f32[512,128]{1,0:T(8,128)}) conditional(s32[]{:T(128)} %convert_element_type.21, (f32[256,128]{1,0:T(8,128)S(1)}, f32[256,128]{1,0:T(8,128)S(1)}) %tuple.149, (f32[256,128]{1,0:T(8,128)S(1)}, f32[256,128]{1,0:T(8,128)S(1)}, s32[1]{0:T(128)}, s32[]{:T(128)}, s32[]{:T(128)}, /*index=5*/s32[]{:T(128)}, pred[]{:T(512)}, ...), branch_computations={%region_6.6_spmd, %region_7.9_spmd} | conditional | flops 125566744 | bytes 1767995 | solution.py:82
  742.2 10.1 %while.61 = (s32[]{:T(128)}, f32[512,128]{1,0:T(8,128)}, s32[]{:T(128)}, s32[]{:T(128)}, s32[]{:T(128)}, /*index=5*/f32[2,255,128]{2,1,0:T(8,128)S(1)}, f32[2,12...) while((s32[]{:T(128)}, f32[512,128]{1,0:T(8,128)}, ...), condition=%wide.region_9.8_spmd, body=%wide.region_8.7_spmd.sunk | while | flops 125501192 | bytes 1243419 | solution.py:77
  745.5 1.7 dynamic_update_slice.10
  750.6 1.6 dynamic_update_slice.10
  754.5 1.9 collective-permute-done.1
  (127 shorter events, 103.3 us)
Async XLA Ops:
  8.2 389.8 %copy-start.1 = (f32[256,128]{1,0:T(8,128)S(1)}, f32[256,128]{1,0:T(8,128)}, u32[]{:S(2)}) copy-start(f32[256,128]{1,0:T(8,128)} %param.21) | copy-start | bytes 393220
  8.2 91.3 %all-gather.5.cloned.1.call-start = ((), (), s32[]{:S(2)}) async-start(), calls=%async_computation.1 | async-start | bytes 2162688 | tf_op jit(solution)/shard_map/while/body/eval_jaxpr/all_gather | solution.py:11
  11.0 192.6 %all-gather.3.cloned.1.call-start = ((), (), s32[]{:S(2)}) async-start(), calls=%async_computation | async-start | bytes 4325376 | tf_op jit(solution)/shard_map/while/body/eval_jaxpr/all_gather | solution.py:11
  206.8 84.1 %all-gather.5.cloned.1.call-start = ((), (), s32[]{:S(2)}) async-start(), calls=%async_computation.1 | async-start | bytes 2162688 | tf_op jit(solution)/shard_map/while/body/eval_jaxpr/all_gather | solution.py:11
  209.6 185.3 %all-gather.3.cloned.1.call-start = ((), (), s32[]{:S(2)}) async-start(), calls=%async_computation | async-start | bytes 4325376 | tf_op jit(solution)/shard_map/while/body/eval_jaxpr/all_gather | solution.py:11
  398.1 3.9 collective-permute-start
  403.6 4.3 collective-permute-start.1
  408.8 6.6 collective-permute-start
  417.0 4.3 collective-permute-start.1
  422.2 6.6 collective-permute-start
  430.4 4.3 collective-permute-start.1
  435.7 6.8 collective-permute-start
  444.1 4.3 collective-permute-start.1
  449.3 7.5 collective-permute-start
  458.4 4.3 collective-permute-start.1
  463.7 7.5 collective-permute-start
  472.8 4.3 collective-permute-start.1
  478.0 7.5 collective-permute-start
  487.1 4.3 collective-permute-start.1
  492.3 7.5 collective-permute-start
  501.4 4.3 collective-permute-start.1
  506.6 7.5 collective-permute-start
  515.7 11.0 %collective-permute-start.1 = (f32[256,128]{1,0:T(8,128)S(1)}, f32[256,128]{1,0:T(8,128)S(1)}, u32[]{:S(2)}, u32[]{:S(2)}) collective-permute-start(f32[256,128]{1,0:T(8,128)S(1)} %slice.110), channel_id=1, source_target_pairs={{0,32},{32,64},{64,96},{96,128},{128,160},{160,192},{192,224},{224... | collective-permute-start | bytes 393224 | tf_op jit(solution)/shard_map/while/body/eval_jaxpr/ppermute | solution.py:17
  527.7 18.9 %collective-permute-start = (f32[256,128]{1,0:T(8,128)S(1)}, f32[256,128]{1,0:T(8,128)S(1)}, u32[]{:S(2)}, u32[]{:S(2)}) collective-permute-start(f32[256,128]{1,0:T(8,128)S(1)} %get-tuple-element.967), channel_id=1, source_target_pairs={{32,0},{64,32},{96,64},{128,96},{160,128},{192,160},{224,192},{256... | collective-permute-start | bytes 393224 | tf_op jit(solution)/shard_map/while/body/eval_jaxpr/ppermute | solution.py:17
  548.2 13.0 %collective-permute-start.1 = (f32[256,128]{1,0:T(8,128)S(1)}, f32[256,128]{1,0:T(8,128)S(1)}, u32[]{:S(2)}, u32[]{:S(2)}) collective-permute-start(f32[256,128]{1,0:T(8,128)S(1)} %slice.110), channel_id=1, source_target_pairs={{0,32},{32,64},{64,96},{96,128},{128,160},{160,192},{192,224},{224... | collective-permute-start | bytes 393224 | tf_op jit(solution)/shard_map/while/body/eval_jaxpr/ppermute | solution.py:17
  562.2 18.8 %collective-permute-start = (f32[256,128]{1,0:T(8,128)S(1)}, f32[256,128]{1,0:T(8,128)S(1)}, u32[]{:S(2)}, u32[]{:S(2)}) collective-permute-start(f32[256,128]{1,0:T(8,128)S(1)} %get-tuple-element.967), channel_id=1, source_target_pairs={{32,0},{64,32},{96,64},{128,96},{160,128},{192,160},{224,192},{256... | collective-permute-start | bytes 393224 | tf_op jit(solution)/shard_map/while/body/eval_jaxpr/ppermute | solution.py:17
  582.6 13.3 %collective-permute-start.1 = (f32[256,128]{1,0:T(8,128)S(1)}, f32[256,128]{1,0:T(8,128)S(1)}, u32[]{:S(2)}, u32[]{:S(2)}) collective-permute-start(f32[256,128]{1,0:T(8,128)S(1)} %slice.110), channel_id=1, source_target_pairs={{0,32},{32,64},{64,96},{96,128},{128,160},{160,192},{192,224},{224... | collective-permute-start | bytes 393224 | tf_op jit(solution)/shard_map/while/body/eval_jaxpr/ppermute | solution.py:17
  596.8 18.4 %collective-permute-start = (f32[256,128]{1,0:T(8,128)S(1)}, f32[256,128]{1,0:T(8,128)S(1)}, u32[]{:S(2)}, u32[]{:S(2)}) collective-permute-start(f32[256,128]{1,0:T(8,128)S(1)} %get-tuple-element.967), channel_id=1, source_target_pairs={{32,0},{64,32},{96,64},{128,96},{160,128},{192,160},{224,192},{256... | collective-permute-start | bytes 393224 | tf_op jit(solution)/shard_map/while/body/eval_jaxpr/ppermute | solution.py:17
  616.8 13.5 %collective-permute-start.1 = (f32[256,128]{1,0:T(8,128)S(1)}, f32[256,128]{1,0:T(8,128)S(1)}, u32[]{:S(2)}, u32[]{:S(2)}) collective-permute-start(f32[256,128]{1,0:T(8,128)S(1)} %slice.110), channel_id=1, source_target_pairs={{0,32},{32,64},{64,96},{96,128},{128,160},{160,192},{192,224},{224... | collective-permute-start | bytes 393224 | tf_op jit(solution)/shard_map/while/body/eval_jaxpr/ppermute | solution.py:17
  631.3 18.2 %collective-permute-start = (f32[256,128]{1,0:T(8,128)S(1)}, f32[256,128]{1,0:T(8,128)S(1)}, u32[]{:S(2)}, u32[]{:S(2)}) collective-permute-start(f32[256,128]{1,0:T(8,128)S(1)} %get-tuple-element.967), channel_id=1, source_target_pairs={{32,0},{64,32},{96,64},{128,96},{160,128},{192,160},{224,192},{256... | collective-permute-start | bytes 393224 | tf_op jit(solution)/shard_map/while/body/eval_jaxpr/ppermute | solution.py:17
  651.1 13.8 %collective-permute-start.1 = (f32[256,128]{1,0:T(8,128)S(1)}, f32[256,128]{1,0:T(8,128)S(1)}, u32[]{:S(2)}, u32[]{:S(2)}) collective-permute-start(f32[256,128]{1,0:T(8,128)S(1)} %slice.110), channel_id=1, source_target_pairs={{0,32},{32,64},{64,96},{96,128},{128,160},{160,192},{192,224},{224... | collective-permute-start | bytes 393224 | tf_op jit(solution)/shard_map/while/body/eval_jaxpr/ppermute | solution.py:17
  665.9 17.8 %collective-permute-start = (f32[256,128]{1,0:T(8,128)S(1)}, f32[256,128]{1,0:T(8,128)S(1)}, u32[]{:S(2)}, u32[]{:S(2)}) collective-permute-start(f32[256,128]{1,0:T(8,128)S(1)} %get-tuple-element.967), channel_id=1, source_target_pairs={{32,0},{64,32},{96,64},{128,96},{160,128},{192,160},{224,192},{256... | collective-permute-start | bytes 393224 | tf_op jit(solution)/shard_map/while/body/eval_jaxpr/ppermute | solution.py:17
  685.4 14.1 %collective-permute-start.1 = (f32[256,128]{1,0:T(8,128)S(1)}, f32[256,128]{1,0:T(8,128)S(1)}, u32[]{:S(2)}, u32[]{:S(2)}) collective-permute-start(f32[256,128]{1,0:T(8,128)S(1)} %slice.110), channel_id=1, source_target_pairs={{0,32},{32,64},{64,96},{96,128},{128,160},{160,192},{192,224},{224... | collective-permute-start | bytes 393224 | tf_op jit(solution)/shard_map/while/body/eval_jaxpr/ppermute | solution.py:17
  700.4 17.7 %collective-permute-start = (f32[256,128]{1,0:T(8,128)S(1)}, f32[256,128]{1,0:T(8,128)S(1)}, u32[]{:S(2)}, u32[]{:S(2)}) collective-permute-start(f32[256,128]{1,0:T(8,128)S(1)} %get-tuple-element.967), channel_id=1, source_target_pairs={{32,0},{64,32},{96,64},{128,96},{160,128},{192,160},{224,192},{256... | collective-permute-start | bytes 393224 | tf_op jit(solution)/shard_map/while/body/eval_jaxpr/ppermute | solution.py:17
  719.7 14.4 %collective-permute-start.1 = (f32[256,128]{1,0:T(8,128)S(1)}, f32[256,128]{1,0:T(8,128)S(1)}, u32[]{:S(2)}, u32[]{:S(2)}) collective-permute-start(f32[256,128]{1,0:T(8,128)S(1)} %slice.110), channel_id=1, source_target_pairs={{0,32},{32,64},{64,96},{96,128},{128,160},{160,192},{192,224},{224... | collective-permute-start | bytes 393224 | tf_op jit(solution)/shard_map/while/body/eval_jaxpr/ppermute | solution.py:17
  735.0 6.4 collective-permute-start
  753.2 3.2 collective-permute-start.1
  757.3 0.7 copy-start
Sparse Core Ops, SparseCore 0:
  12.3 87.2 all-gather.4
  102.7 100.9 all-gather.2
  210.8 80.0 all-gather.4
  293.9 100.9 all-gather.2
